TPU v7x, 32 devices: a whole 2x2x4 slice. The times are simulated.
32 devices in a mesh: rows: 8 (over z, x), feat: 4 (over y, core).
Axes of the slice: x: 2, y: 2, z: 4, core: 2. Of those that a mesh axis runs over, the one named last changes fastest.
Arguments:
- slab_rows: bfloat16 [4096, 2048], P('rows', 'feat'), may hold values from -0.125 to 0.125
- labels: int32 [4096], P('rows'), may hold values 0 or 1
- center: float32 [2048], P('feat'), may hold values from -4 to 4
- theta_start: float32 [64, 2048], P(None, 'feat'), may hold values from -4 to 4
- momentum: float32 [64, 2048], P(None, 'feat'), may hold values from -6 to 6
- step_size: float32 [64], replicated, may hold values from 0.5 to 2
- sample_index: int32 [8192], P('rows'), may hold values from 0 to 511
- sample_count: int32 [8], P('rows'), may hold values from 128 to 1024, as said below
Outputs:
- theta_end: float32 [64, 2048], P(None, 'feat')
- momentum_end: float32 [64, 2048], P(None, 'feat')
- hessian: float32 [2048, 2048], P('feat', 'rows')
Inputs may be any that keep to these rules, and one draw needn't show every extreme that they name: `sample_index`: row numbers in slots that are not live are arbitrary and unused. `sample_count`: A multiple of 128; some index of rows holds exactly 1024 live slots.
All inputs are finite; a program needn't handle non-finite values. No bound on the sum of `labels` on one device may be relied on, other than what follows from the above.
Results may differ from a plain program's by a relative error of at most 0.0063.
Values may be sent and summed in bfloat16 or wider, within the bound.
A program may use at most 64 MiB of HBM per device.

v0:
```python
import math

import jax
import jax.numpy as jnp
from jax import lax
from jax.sharding import PartitionSpec as P

D = 2048
STEPS = 2
SUB_BLOCK = 128


def shards(slab_rows, labels, center, theta_start, momentum, step_size, sample_index, sample_count):
    whole_rows = slab_rows.shape[0] * lax.axis_size("rows")
    chains = theta_start.shape[0]
    capacity = sample_index.shape[0]
    width_own = slab_rows.shape[1]
    full_width = width_own * lax.axis_size("feat")
    column_width = full_width // lax.axis_size("rows")
    column_start = lax.axis_index("rows") * column_width
    center_bf = center.astype(jnp.bfloat16)
    partial_value = jnp.dot(slab_rows, center_bf, preferred_element_type=jnp.float32)
    logit_hat = lax.psum(partial_value, "feat")
    prob_hat = jax.nn.sigmoid(logit_hat)
    weight = prob_hat * (1.0 - prob_hat)
    residual = labels.astype(jnp.float32) - prob_hat
    scaled = (weight[:, None] * slab_rows).astype(jnp.bfloat16)
    hessian_block = lax.dot_general(
        scaled,
        lax.all_gather(slab_rows, "feat", axis=1, tiled=True),
        (((0,), (0,)), ((), ())),
        preferred_element_type=jnp.float32,
    )
    grad_local = jnp.dot(
        residual.astype(jnp.bfloat16), slab_rows, preferred_element_type=jnp.float32
    )
    live_rows = sample_count[0]
    count_float = live_rows.astype(jnp.float32)
    hessian_out = lax.psum_scatter(hessian_block, "rows", scatter_dimension=1, tiled=True)
    grad_hat, sample_total = lax.psum((grad_local, count_float), "rows")
    weight_ratio = whole_rows / sample_total
    picked = jnp.take(slab_rows, sample_index, axis=0)
    logit_ref = jnp.take(logit_hat, sample_index)
    prob_ref = jax.nn.sigmoid(logit_ref)
    weight_ref = prob_ref * (1.0 - prob_ref)
    live_blocks = live_rows // SUB_BLOCK
    center_full = lax.all_gather(center, "feat", axis=0, tiled=True)
    leap_size = step_size[:, None] * math.sqrt(D / whole_rows)

    def logit_blocks(operand, position_bf):

        def add_block(number, buffer):
            first_row = number * SUB_BLOCK
            rows_here = lax.dynamic_slice_in_dim(operand, first_row, SUB_BLOCK, 0)
            values = lax.dot_general(
                rows_here, position_bf, (((1,), (1,)), ((), ())), preferred_element_type=jnp.float32
            )
            return lax.dynamic_update_slice_in_dim(buffer, values, first_row, 0)

        return lax.fori_loop(0, live_blocks, add_block, jnp.zeros((capacity, chains), jnp.float32))

    def gradient(position):
        position_full = lax.all_gather(
            position.astype(jnp.bfloat16), "feat", axis=1, tiled=True
        ).astype(position.dtype)
        offset_full = position_full - center_full[None, :]
        logit_now = lax.psum(
            logit_blocks(picked, position.astype(jnp.bfloat16)).astype(jnp.bfloat16), "feat"
        ).astype(jnp.float32)

        def add_term(number, accum_sum):
            first_row = number * SUB_BLOCK
            current = lax.dynamic_slice_in_dim(logit_now, first_row, SUB_BLOCK, 0)
            anchor = lax.dynamic_slice_in_dim(logit_ref, first_row, SUB_BLOCK, 0)[:, None]
            anchor_prob = lax.dynamic_slice_in_dim(prob_ref, first_row, SUB_BLOCK, 0)[:, None]
            anchor_weight = lax.dynamic_slice_in_dim(weight_ref, first_row, SUB_BLOCK, 0)[:, None]
            remainder = anchor_prob - jax.nn.sigmoid(current) + anchor_weight * (current - anchor)
            remainder = remainder.astype(jnp.bfloat16)
            rows_here = lax.dynamic_slice_in_dim(picked, first_row, SUB_BLOCK, 0)
            return accum_sum + lax.dot_general(
                remainder, rows_here, (((0,), (0,)), ((), ())), preferred_element_type=jnp.float32
            )

        correction = lax.fori_loop(
            0, live_blocks, add_term, jnp.zeros((chains, width_own), jnp.float32)
        )
        offset_cols = lax.dynamic_slice_in_dim(offset_full, column_start, column_width, 1)
        curvature = 0.0
        curv_part = lax.dot_general(
            offset_cols,
            hessian_out,
            (((1,), (1,)), ((), ())),
            precision=lax.Precision.HIGHEST,
            preferred_element_type=jnp.float32,
        )
        summand = weight_ratio * correction - curv_part
        combined = lax.psum(summand, "rows")
        return grad_hat[None, :] - curvature + combined - position

    position = theta_start
    moment = momentum + 0.5 * leap_size * gradient(position)
    for leap_index in range(STEPS):
        position = position + leap_size * moment
        factor = leap_size if leap_index + 1 < STEPS else 0.5 * leap_size
        moment = moment + factor * gradient(position)
    return (position, moment, hessian_out)


def solution(mesh):
    return jax.shard_map(
        shards,
        mesh=mesh,
        in_specs=(
            P("rows", "feat"),
            P("rows"),
            P("feat"),
            P(None, "feat"),
            P(None, "feat"),
            P(),
            P("rows"),
            P("rows"),
        ),
        out_specs=(P(None, "feat"), P(None, "feat"), P("feat", "rows")),
        check_vma=False,
    )
```

profile of v0, /device:TPU:0, one launch (start us, length us, event | category | flops | bytes accessed | tf_op | source)
XLA Modules:
  0.0 460.8 jit_solution(4636648141346456119)
XLA Ops:
  7.2 0.7 all-gather.3.cloned.1.call-update
  8.0 0.7 convert_element_type.67
  9.3 0.7 fusion.42
  10.0 4.0 gather_fusion.1
  14.0 0.2 fusion.47
  14.2 8.4 %psum.63 = f32[512]{0:T(512)S(1)} all-reduce(f32[512]{0:T(512)S(1)} %bitcast.29), channel_id=1, replica_groups=mesh['rows'=8,'feat'=4] {'feat'}, use_global_device_ids=true, to_apply=%region_0.0 | all-reduce | flops 512 | bytes 4096 | tf_op jit(solution)/shard_map/psum | solution.py:23
  22.6 6.9 %gather_fusion = f32[1024]{0:T(1024)S(1)} fusion(f32[512]{0:T(512)S(1)} %psum.63, s32[1024]{0:T(1024)S(1)} %fusion.42), kind=kCustom, calls=%fused_computation | custom fusion | bytes 12288 | tf_op jit(solution)/shard_map/jit(_take)/gather | solution.py:43
  29.6 0.2 broadcast_select_fusion
  29.8 0.2 while.60
  29.8 0.2 convolution_dynamic-update-slice_fusion.6
  30.0 0.6 copy-done.3
  30.7 0.0 reduce-scatter.2.cloned.1.call-start
  30.8 4.2 all-gather.3.cloned.1.call-done
  34.9 4.9 %fusion.27 = f32[512,2048]{1,0:T(8,128)} fusion(bf16[512,2048]{1,0:T(8,128)(2,1)} %all-gather.3.cloned.1.call-done, bf16[512,512]{1,0:T(8,128)(2,1)S(1)} %copy-done, f32[512]{0:T(512)S(1)} %get-tuple-element.334), kind=kOutput, calls=%fused_computation.46 | convolution fusion | flops 1074528256 | bytes 6817792 | tf_op jit(solution)/shard_map/dot_general | solution.py:28
  39.9 0.0 all-reduce.10.cloned.1.call-start
  39.9 0.2 fusion.48
  40.1 21.9 %all-reduce = (f32[]{:T(128)}, f32[512]{0:T(512)S(1)}) all-reduce(f32[]{:T(128)S(6)} %convert_element_type.69, f32[512]{0:T(512)S(1)} %bitcast.28), channel_id=1, replica_groups=mesh['rows'=8,'feat'=4] {'rows'}, use_global_device_ids=true, to_apply=%region_2.0 | all-reduce | flops 513 | bytes 4104 | tf_op jit(solution)/shard_map/psum | solution.py:40
  62.8 5.2 %all-gather = f32[4,1,512]{2,1,0:T(1,128)S(1)} all-gather(f32[1,1,512]{2,1,0:T(1,128)S(1)} %bitcast.30), channel_id=1, replica_groups=mesh['rows'=8,'feat'=4] {'feat'}, dimensions={0}, use_global_device_ids=true | all-gather | bytes 10240 | tf_op jit(solution)/shard_map/all_gather | solution.py:47
  67.9 0.1 dynamic-slice
  68.0 5.8 %all_gather.15 = bf16[64,2048]{1,0:T(8,128)(2,1)S(1)} all-gather(bf16[64,512]{1,0:T(8,128)(2,1)S(1)} %get-tuple-element.790), channel_id=1, replica_groups=mesh['rows'=8,'feat'=4] {'feat'}, dimensions={1}, use_global_device_ids=true | all-gather | bytes 327680 | tf_op jit(solution)/shard_map/all_gather | solution.py:63
  73.8 0.9 convert_element_type.72
  74.8 0.7 while.61
  74.8 0.1 copy.29
  74.9 0.1 dynamic_slice.117
  75.0 0.1 dynamic_slice.118
  75.1 0.1 dynamic_slice.119
  75.2 0.3 convolution_add_fusion.6
  75.5 87.0 %reduce-scatter.2.cloned.1.call-done = f32[512,256]{1,0:T(8,128)} async-done(((f32[512,2048]{1,0:T(8,128)}), f32[512,256]{1,0:T(8,128)}) %reduce-scatter.2.cloned.1.call-update) | async-done | bytes 524304 | tf_op jit(solution)/shard_map/reduce_scatter | solution.py:39
  162.4 2.3 convolution_subtract_fusion.2
  164.8 0.0 all-reduce.12.cloned.1.call-start
  164.8 70.9 %all-reduce.10.cloned.1.call-done = f32[64,512]{1,0:T(8,128)} async-done(((f32[64,512]{1,0:T(8,128)}), f32[64,512]{1,0:T(8,128)}) %all-reduce.10.cloned.1.call-update) | async-done | bytes 131088 | tf_op jit(solution)/shard_map/psum | solution.py:97
  235.7 1.0 fusion.41
  236.7 0.2 while.62
  236.7 0.2 convolution_dynamic-update-slice_fusion.7
  236.9 0.6 copy-done.4
  237.6 0.0 all-reduce.14.cloned.1.call-start
  237.7 5.9 %all_gather.18 = bf16[64,2048]{1,0:T(8,128)(2,1)S(1)} all-gather(bf16[64,512]{1,0:T(8,128)(2,1)S(1)} %get-tuple-element.791), channel_id=1, replica_groups=mesh['rows'=8,'feat'=4] {'feat'}, dimensions={1}, use_global_device_ids=true | all-gather | bytes 327680 | tf_op jit(solution)/shard_map/all_gather | solution.py:63
  243.6 25.6 %all-reduce.12.cloned.1.call-done = bf16[1024,64]{0,1:T(8,128)(2,1)} async-done(((bf16[1024,64]{0,1:T(8,128)(2,1)}), bf16[1024,64]{0,1:T(8,128)(2,1)}) %all-reduce.12.cloned.1.call-update) | async-done | bytes 131088 | tf_op jit(solution)/shard_map/psum | solution.py:67
  269.2 0.9 convert_element_type.78
  270.2 0.7 while.63
  270.2 0.1 copy.30
  270.3 0.1 dynamic_slice.123
  270.4 0.1 dynamic_slice.124
  270.5 0.1 dynamic_slice.125
  270.5 0.3 convolution_add_fusion.7
  270.8 1.3 convolution_subtract_fusion.1
  272.2 71.7 %all-reduce.14.cloned.1.call-done = f32[64,512]{1,0:T(8,128)} async-done(((f32[64,512]{1,0:T(8,128)}), f32[64,512]{1,0:T(8,128)}) %all-reduce.14.cloned.1.call-update) | async-done | bytes 131088 | tf_op jit(solution)/shard_map/psum | solution.py:97
  343.9 1.0 fusion.46
  345.0 0.2 while.64
  345.0 0.2 convolution_dynamic-update-slice_fusion.8
  345.2 0.6 copy-done.5
  345.9 0.0 all-reduce.18.cloned.1.call-start
  345.9 5.8 %all_gather.19 = bf16[64,2048]{1,0:T(8,128)(2,1)S(1)} all-gather(bf16[64,512]{1,0:T(8,128)(2,1)S(1)} %get-tuple-element.792), channel_id=1, replica_groups=mesh['rows'=8,'feat'=4] {'feat'}, dimensions={1}, use_global_device_ids=true | all-gather | bytes 327680 | tf_op jit(solution)/shard_map/all_gather | solution.py:63
  351.7 25.9 %all-reduce.16.cloned.1.call-done = bf16[1024,64]{0,1:T(8,128)(2,1)} async-done(((bf16[1024,64]{0,1:T(8,128)(2,1)}), bf16[1024,64]{0,1:T(8,128)(2,1)}) %all-reduce.16.cloned.1.call-update) | async-done | bytes 131088 | tf_op jit(solution)/shard_map/psum | solution.py:67
  377.6 0.9 convert_element_type.82
  378.6 0.7 while.65
  378.6 0.1 copy.31
  378.7 0.1 dynamic_slice.129
  378.8 0.1 dynamic_slice.130
  378.8 0.1 dynamic_slice.131
  378.9 0.3 convolution_add_fusion.8
  379.2 1.3 convolution_subtract_fusion
  380.5 71.8 %all-reduce.18.cloned.1.call-done = f32[64,512]{1,0:T(8,128)} async-done(((f32[64,512]{1,0:T(8,128)}), f32[64,512]{1,0:T(8,128)}) %all-reduce.18.cloned.1.call-update) | async-done | bytes 131088 | tf_op jit(solution)/shard_map/psum | solution.py:97
  452.3 1.7 multiply_add_fusion
  (50 shorter events, 0.5 us)
Async XLA Ops:
  7.2 2.8 copy-start
  7.2 27.8 %all-gather.3.cloned.1.call-start = ((), (), s32[]{:S(2)}) async-start(), calls=%async_computation.2 | async-start | bytes 2621440 | tf_op jit(solution)/shard_map/all_gather | solution.py:30
  7.9 65.9 %all-reduce.8.cloned.1.call-start = ((), (), s32[]{:S(2)}) async-start(), calls=%async_computation.1 | async-start | bytes 262144 | tf_op jit(solution)/shard_map/psum | solution.py:67
  22.6 6.9 %copy-start.2 = (f32[64,512]{1,0:T(8,128)S(1)}, f32[64,512]{1,0:T(8,128)}, u32[]{:S(2)}) copy-start(f32[64,512]{1,0:T(8,128)} %param.23) | copy-start | bytes 393220
  22.6 6.9 %copy-start.9 = (s32[1024]{0:T(1024)S(1)}, s32[1024]{0:T(1024)}, u32[]{:S(2)}) copy-start(s32[1024]{0:T(1024)} %param.26) | copy-start | bytes 12292
  29.5 1.3 copy-start.11
  30.0 0.7 copy-start.3
  30.7 131.7 %reduce-scatter.2.cloned.1.call-start = ((), (), s32[]{:S(2)}) async-start(), calls=%async_computation.3 | async-start | bytes 4718592 | tf_op jit(solution)/shard_map/reduce_scatter | solution.py:39
  39.8 22.9 %copy-start.10 = (f32[512]{0:T(512)S(1)}, f32[512]{0:T(512)}, u32[]{:S(2)}) copy-start(f32[512]{0:T(512)} %param.22) | copy-start | bytes 6148
  39.9 195.8 %all-reduce.10.cloned.1.call-start = ((), (), s32[]{:S(2)}) async-start(), calls=%async_computation.4 | async-start | bytes 262144 | tf_op jit(solution)/shard_map/psum | solution.py:97
  74.8 90.0 %copy-start.12 = (f32[64]{0:T(128)S(1)}, f32[64]{0:T(128)}, u32[]{:S(2)}) copy-start(f32[64]{0:T(128)} %param.25) | copy-start | bytes 772
  74.8 160.9 %copy-start.8 = (f32[64,512]{1,0:T(8,128)S(1)}, f32[64,512]{1,0:T(8,128)}, u32[]{:S(2)}) copy-start(f32[64,512]{1,0:T(8,128)} %param.24) | copy-start | bytes 393220
  164.8 104.5 %all-reduce.12.cloned.1.call-start = ((), (), s32[]{:S(2)}) async-start(), calls=%async_computation.5 | async-start | bytes 262144 | tf_op jit(solution)/shard_map/psum | solution.py:67
  236.9 0.7 copy-start.4
  237.6 33.2 %copy-start.1 = (f32[512,256]{1,0:T(8,128)S(1)}, f32[512,256]{1,0:T(8,128)}, u32[]{:S(2)}) copy-start(f32[512,256]{1,0:T(8,128)} %reduce-scatter.2.cloned.1.call-done) | copy-start | bytes 1572868
  237.6 106.3 %all-reduce.14.cloned.1.call-start = ((), (), s32[]{:S(2)}) async-start(), calls=%async_computation.6 | async-start | bytes 262144 | tf_op jit(solution)/shard_map/psum | solution.py:97
  272.2 105.4 %all-reduce.16.cloned.1.call-start = ((), (), s32[]{:S(2)}) async-start(), calls=%async_computation.7 | async-start | bytes 262144 | tf_op jit(solution)/shard_map/psum | solution.py:67
  344.9 107.4 %copy-start.7 = (f32[64,512]{1,0:T(8,128)}, f32[64,512]{1,0:T(8,128)S(1)}, u32[]{:S(2)}) copy-start(f32[64,512]{1,0:T(8,128)S(1)} %get-tuple-element.327) | copy-start | bytes 393220
  345.2 0.7 copy-start.5
  345.9 106.5 %all-reduce.18.cloned.1.call-start = ((), (), s32[]{:S(2)}) async-start(), calls=%async_computation.8 | async-start | bytes 262144 | tf_op jit(solution)/shard_map/psum | solution.py:97
  378.5 73.8 %copy-start.6 = (f32[64,512]{1,0:T(8,128)S(1)}, f32[64,512]{1,0:T(8,128)}, u32[]{:S(2)}) copy-start(f32[64,512]{1,0:T(8,128)} %all-reduce.14.cloned.1.call-done) | copy-start | bytes 393220
Sparse Core Ops, SparseCore 0:
  9.6 25.3 all-gather.2
  37.8 31.3 all-reduce.7
  73.9 88.4 reduce-scatter.1
  166.2 69.4 all-reduce.9
  238.5 30.6 all-reduce.11
  273.0 70.8 all-reduce.13
  346.9 30.6 all-reduce.15
  381.5 70.7 all-reduce.17
where the time goes:
time: 465 us; the launch traced here: 461 us
  waiting for transfers between devices  358 us (77%)
  blocking collectives  53 us (11%)
  between operations  15.8 us (3%)
  local copies, waits for them, and re-layouts  14 us (3%)
  matrix products  11.6 us (2%)
  other arithmetic  8.08 us (2%)
    psum x3, waiting for transfers between devices, gradient(): combined = lax.psum(summand, 'rows')  214 us
    reduce_scatter x1, waiting for transfers between devices, shards(): lax.psum_scatter(hessian_block, 'rows', scatter_dimension=1, tiled=True)  87 us
    psum x3, waiting for transfers between devices, gradient(): lax.psum(logit_blocks(picked, position.astype(jnp.bfloat16)).astype(jnp.b...  51.5 us
    psum x1, blocking collectives, shards(): grad_hat, sample_total = lax.psum((grad_local, count_float), 'rows')  21.9 us
    all_gather x3, blocking collectives, gradient(): lax.all_gather(position.astype(jnp.bfloat16), 'feat', axis=1, tiled=True)  17.5 us
  transfers between devices with their start and end apart: 8, of which 7 were waited for; matrix products, arithmetic and copies ran while one was open for 4% of the time, Pallas kernels for 0%

commit v1 on v0

v1 whole, which is shorter than its diff:
```python
import functools
import math

import jax
import jax.numpy as jnp
from jax import lax
from jax.experimental import pallas as pl
from jax.experimental.pallas import tpu as pltpu
from jax.sharding import PartitionSpec as P

STEPS = 2
LANES = 128
PIECES = 4
MESH = pl.DeviceIdType.MESH
F32, BF16 = jnp.float32, jnp.bfloat16


def each(count, body, limit=8):
    if count <= limit:
        for number in range(count):
            body(number)
    else:
        lax.fori_loop(0, count, lambda number, none: (body(number), none)[1], 0)


def dot(left, right, left_dim, right_dim):
    return lax.dot_general(
        left, right, (((left_dim,), (right_dim,)), ((), ())), preferred_element_type=F32
    )


def split(value):
    high = value.astype(BF16)
    return high, (value - high.astype(F32)).astype(BF16)


def kernel(
    R, F, S, whole_rows,
    x_ref, label_ref, mult_ref, count_ref, center_ref, theta_ref, mom_ref, leap_ref,
    theta_out, mom_out, hess_out,
    x_full, theta_full, mom_full, center_full, count_full,
    c_send, c_recv, state, state_recv, final_recv,
    h_part, h_send, h_recv, h_send2, h_recv2,
    x_ssem, x_rsem, x_fsem, s_ssem, s_rsem, n_ssem, n_rsem,
    c_ssem, c_rsem, p_ssem, p_rsem, o_ssem, o_rsem,
    h_ssem, h_rsem, g_ssem, g_rsem,
):
    rows, wide = x_ref.shape
    group = theta_ref.shape[0] // F
    w = c_send.shape[-1]
    per = wide // w
    A = R // 2
    cw = hess_out.shape[0]
    r, f = lax.axis_index("rows"), lax.axis_index("feat")
    a, b = r // 2, lax.rem(r, 2)
    mate = f + 1 - 2 * lax.rem(f, 2)
    piece = rows // PIECES

    def copy(src, dst, ssem, rsem, row, feat):
        return pltpu.make_async_remote_copy(
            src_ref=src, dst_ref=dst, send_sem=ssem, recv_sem=rsem,
            device_id=(row, feat), device_id_type=MESH,
        )

    def row_peer(i):
        return lax.rem(r + i + 1, R)

    barrier = pltpu.get_barrier_semaphore()

    def greet_row(i):
        pl.semaphore_signal(barrier, inc=1, device_id=(row_peer(i), f), device_id_type=MESH)

    def greet_feat(i):
        pl.semaphore_signal(
            barrier, inc=1, device_id=(r, lax.rem(f + i + 1, F)), device_id_type=MESH
        )

    each(R - 1, greet_row)
    each(F - 1, greet_feat)
    pl.semaphore_wait(barrier, R + F - 2)

    def small(i, number):
        peer = lax.rem(f + i + 1, F)
        theirs = pl.ds(pl.multiple_of(peer * group, group), group)
        src = (center_ref, theta_ref.at[theirs], mom_ref.at[theirs])[number]
        dst = (center_full, theta_full, mom_full)[number].at[f]
        return copy(src, dst, s_ssem.at[number, peer], s_rsem.at[number, f], r, peer)

    def small_in(i, number):
        peer = lax.rem(f + i + 1, F)
        dst = (center_full, theta_full, mom_full)[number].at[peer]
        return copy(dst, dst, s_ssem.at[number, peer], s_rsem.at[number, peer], r, peer)

    def part(c):
        return pl.ds(c * piece, piece)

    def x_out(i, c):
        peer = mate if i == 0 else lax.rem(f + 2 * i, F)
        return copy(
            x_ref.at[part(c)], x_full.at[f, part(c)], x_ssem.at[i, c], x_rsem.at[f, c], r, peer
        )

    def x_in(block, c):
        dst = x_full.at[block, part(c)]
        return copy(dst, dst, x_ssem.at[0, c], x_rsem.at[block, c], r, mate)

    def x_forward(i, c):
        block = lax.rem(f + 2 * i, F)
        dst = x_full.at[block, part(c)]
        return copy(dst, dst, x_fsem.at[i, c], x_rsem.at[block, c], r, mate)

    def count_out(i):
        peer = row_peer(i)
        return copy(count_ref, count_full.at[r], n_ssem.at[peer], n_rsem.at[r], peer, f)

    def count_in(i):
        peer = row_peer(i)
        dst = count_full.at[peer]
        return copy(dst, dst, n_ssem.at[peer], n_rsem.at[peer], peer, f)

    for c in range(PIECES):
        for i in range(1, F // 2):
            x_out(i, c).start()
        if c == 0:
            for i in range(F - 1):
                for number in range(3):
                    small(i, number).start()
            each(R - 1, lambda i: count_out(i).start())
    for c in range(PIECES):
        x_out(0, c).start()

    mine = pl.ds(pl.multiple_of(f * group, group), group)
    center_full[f] = center_ref[...]
    theta_full[f] = theta_ref[mine]
    mom_full[f] = mom_ref[mine]
    x_full[f] = x_ref[...]
    count_full[r] = count_ref[...]
    leap = leap_ref[mine, :]

    for i in range(F - 1):
        for number in range(3):
            small_in(i, number).wait_recv()
    each(R - 1, lambda i: count_in(i).wait_recv())
    total = lax.fori_loop(0, R, lambda i, acc: acc + count_full[i], jnp.zeros_like(count_ref))
    ratio = float(whole_rows) / total[:1, :1]

    for c in range(PIECES):
        for i in range(1, F // 2):
            x_in(lax.rem(f + 2 * i, F), c).wait_recv()
            x_forward(i, c).start()
    for c in range(PIECES):
        x_in(mate, c).wait_recv()
    for c in range(PIECES):
        for i in range(1, F // 2):
            x_in(lax.rem(mate + 2 * i, F), c).wait_recv()

    at_center = jnp.zeros((2 * group, rows), F32)
    for g in range(F):
        high, low = split(center_full[g])
        at_center += dot(jnp.concatenate([high, low], 0), x_full[g], 1, 1)
    logit_hat = at_center[:1]
    center_all = at_center[:1] + at_center[group : group + 1]
    prob_hat = jax.nn.sigmoid(logit_hat)
    weight = prob_hat * (1.0 - prob_hat)
    residual = (label_ref[...] - prob_hat).astype(BF16).astype(F32)
    mult_ratio = mult_ref[...] * ratio

    def c_out(e, i):
        peer = row_peer(i)
        return copy(
            c_send.at[e, lax.rem(peer, S)], c_recv.at[e, r], c_ssem.at[e, peer],
            c_rsem.at[e, r], peer, f,
        )

    def c_in(e, i):
        peer = row_peer(i)
        dst = c_recv.at[e, peer]
        return copy(dst, dst, c_ssem.at[e, peer], c_rsem.at[e, peer], peer, f)

    def on_owner(number, body):
        if S == R:
            body()
        else:
            pl.when(number < S)(body)

    def contribute(e, chunk_of):
        now = jnp.zeros((2 * group, rows), F32)
        for k in range(S):
            high, low = split(chunk_of(k))
            columns = x_full[k // per, :, (k % per) * w : (k % per + 1) * w]
            now += dot(jnp.concatenate([high, low], 0), columns, 1, 1)
        logit_now = now[:group]
        offset = now[:group] + now[group:] - center_all
        remainder = prob_hat - jax.nn.sigmoid(logit_now) + weight * (logit_now - logit_hat)
        remainder = remainder.astype(BF16).astype(F32)
        coef = residual - weight * offset + mult_ratio * remainder
        high, low = split(coef)
        both = jnp.concatenate([high, low], 0)
        for g in range(F):
            value = dot(both, x_full[g], 1, 0)
            value = value[:group] + value[group:]
            for h in range(per):
                c_send[e, g * per + h] = value[:, h * w : (h + 1) * w]

        def send(i):
            on_owner(row_peer(i), lambda: c_out(e, i).start())

        each(R - 1, send)

    def reduced(e):
        on_owner(r, lambda: each(R - 1, lambda i: c_in(e, i).wait_recv()))
        c_recv[e, r] = c_send[e, lax.rem(r, S)]
        return lax.fori_loop(0, R, lambda i, acc: acc + c_recv[e, i], jnp.zeros((group, w), F32))

    def p_out(e, i):
        peer = row_peer(i)
        own = lax.rem(r, S)
        return copy(
            state.at[e], state_recv.at[e, own], p_ssem.at[e, peer], p_rsem.at[e, own], peer, f
        )

    def p_in(e, i):
        peer = lax.rem(row_peer(i), S)
        dst = state_recv.at[e, peer]
        return copy(dst, dst, p_ssem.at[e, peer], p_rsem.at[e, peer], row_peer(i), f)

    def spread(e):
        each(R - 1, lambda i: p_out(e, i).start())
        state_recv[e, lax.rem(r, S)] = state[e]

    def gathered(e):
        def take(i):
            on_owner(row_peer(i), lambda: p_in(e, i).wait_recv())

        each(R - 1, take)

    def h_out(pair):
        rows_there = pl.ds(pl.multiple_of((2 * pair + 1 - b) * cw, cw), cw)
        return copy(
            h_send.at[rows_there], h_recv.at[pair], h_ssem.at[pair], h_rsem.at[pair],
            2 * a + 1 - b, f,
        )

    def g_out(pair):
        return copy(
            h_send2.at[pair], h_recv2.at[a], g_ssem.at[pair], g_rsem.at[a], 2 * pair + b, f
        )

    def g_in(pair):
        dst = h_recv2.at[pair]
        return copy(dst, dst, g_ssem.at[pair], g_rsem.at[pair], 2 * pair + b, f)

    many = A // F

    def block_at(i):
        return lax.rem(a // many + 1 + i, F)

    def h_start():
        column = jnp.transpose(jnp.broadcast_to(weight, (LANES, rows)))[:, :1]
        scaled = (column * x_ref[...].astype(F32)).astype(BF16)

        for i in range(F):
            g = block_at(i)
            value = dot(x_full[g], scaled, 0, 0)
            where = pl.ds(pl.multiple_of(g * wide, wide), wide)
            h_part[where, :] = value
            h_send[where, :] = value.astype(BF16)
            each(many, lambda j: h_out(g * many + j).start())

    def h_pass(i):
        def one(j):
            pair = block_at(i) * many + j
            h_out(pair).wait_recv()
            own = pl.ds(pl.multiple_of((2 * pair + b) * cw, cw), cw)
            value = h_part[own, :] + h_recv[pair].astype(F32)

            @pl.when(pair == a)
            def _():
                hess_out[...] = value

            @pl.when(pair != a)
            def _():
                h_send2[pair] = value.astype(BF16)
                g_out(pair).start()

        each(many, one)

    def o_out(number, i):
        peer = lax.rem(f + i + 1, F)
        theirs = pl.ds(peer * per, per)
        return copy(
            state_recv.at[STEPS - 1 + number, theirs], final_recv.at[number, f], o_ssem.at[number, peer],
            o_rsem.at[number, f], r, peer,
        )

    def o_in(number, i):
        peer = lax.rem(f + i + 1, F)
        dst = final_recv.at[number, peer]
        return copy(dst, dst, o_ssem.at[number, peer], o_rsem.at[number, peer], r, peer)

    def finish(number):
        for i in range(F - 1):
            o_out(number, i).start()
        for h in range(per):
            final_recv[number, f, h] = state_recv[STEPS - 1 + number, f * per + h]

    def write(number, out):
        for i in range(F - 1):
            o_in(number, i).wait_recv()
        for g in range(F):
            for h in range(per):
                out[g * group : (g + 1) * group, h * w : (h + 1) * w] = final_recv[number, g, h]

    own = lax.rem(r, S)

    def own_part(full):
        block = own // per
        if per == 1:
            return full[block]
        value = full[block, :, :w]
        for h in range(1, per):
            value = jnp.where(
                lax.rem(own, per) == h, full[block, :, h * w : (h + 1) * w], value
            )
        return value

    contribute(
        0, lambda k: theta_full[k // per, :, (k % per) * w : (k % per + 1) * w]
    )
    h_start()
    position, moment = own_part(theta_full), own_part(mom_full)
    factor = 0.5 * leap
    for e in range(STEPS):
        moment = moment + factor * (reduced(e) - position)
        position = position + leap * moment
        factor = leap if e + 1 < STEPS else 0.5 * leap
        state[e] = position
        on_owner(r, functools.partial(spread, e))
        if e + 1 < STEPS or STEPS == 1:
            h_pass(0)
        gathered(e)
        contribute(e + 1, functools.partial(lambda k, e: state_recv[e, k], e=e))
        if e == STEPS - 1:
            finish(0)
        h_pass(1 + e)
    moment = moment + factor * (reduced(STEPS) - position)
    state[STEPS] = moment
    on_owner(r, functools.partial(spread, STEPS))
    for i in range(1 + STEPS, F):
        h_pass(i)
    gathered(STEPS)
    finish(1)
    write(0, theta_out)

    def h_add(i):
        pair = lax.rem(a + 1 + i, A)
        g_in(pair).wait_recv()
        hess_out[...] += h_recv2[pair].astype(F32)

    each(A - 1, h_add)
    write(1, mom_out)

    for c in range(PIECES):
        for i in range(F // 2):
            x_out(i, c).wait_send()
        for i in range(1, F // 2):
            x_forward(i, c).wait_send()
    for i in range(F - 1):
        for number in range(3):
            small(i, number).wait_send()
        for number in range(2):
            o_out(number, i).wait_send()
    each(R - 1, lambda i: count_out(i).wait_send())
    for e in range(STEPS + 1):
        each(
            R - 1,
            lambda i: on_owner(row_peer(i), lambda: c_out(e, i).wait_send()),
        )
        on_owner(r, lambda: each(R - 1, lambda i: p_out(e, i).wait_send()))
    each(A, lambda pair: h_out(pair).wait_send())
    each(A - 1, lambda i: g_out(lax.rem(a + 1 + i, A)).wait_send())


def shards(slab_rows, labels, center, theta_start, momentum, step_size, sample_index, sample_count):
    R, F = lax.axis_size("rows"), lax.axis_size("feat")
    rows, wide = slab_rows.shape
    whole_rows = rows * R
    full = wide * F
    chains = theta_start.shape[0]
    group = chains // F
    S = min(R, full // LANES)
    w = full // S
    cw = full // R
    A = R // 2
    live = jnp.arange(sample_index.shape[0], dtype=jnp.int32) < sample_count[0]
    slot_row = jnp.where(live, sample_index, -1)
    mult = jnp.sum(
        (slot_row[:, None] == jnp.arange(rows, dtype=jnp.int32)[None, :]).astype(F32), axis=0
    )[None, :]
    count = jnp.broadcast_to(sample_count.astype(F32)[None, :], (8, LANES))
    center_rows = jnp.broadcast_to(center[None, :], (group, wide))
    leap = (step_size * math.sqrt(full / whole_rows))[:, None]
    vmem = pl.BlockSpec(memory_space=pltpu.VMEM)
    dma = pltpu.SemaphoreType.DMA
    steps = STEPS + 1
    per = wide // w
    theta, moment, hess = pl.pallas_call(
        functools.partial(kernel, R, F, S, whole_rows),
        out_shape=(
            jax.ShapeDtypeStruct((chains, wide), F32),
            jax.ShapeDtypeStruct((chains, wide), F32),
            jax.ShapeDtypeStruct((cw, wide), F32),
        ),
        in_specs=[vmem] * 8,
        out_specs=(vmem,) * 3,
        scratch_shapes=[
            pltpu.VMEM((F, rows, wide), BF16),
            pltpu.VMEM((F, group, wide), F32),
            pltpu.VMEM((F, group, wide), F32),
            pltpu.VMEM((F, group, wide), F32),
            pltpu.VMEM((R, 8, LANES), F32),
            pltpu.VMEM((steps, S, group, w), F32),
            pltpu.VMEM((steps, R, group, w), F32),
            pltpu.VMEM((steps, group, w), F32),
            pltpu.VMEM((steps, S, group, w), F32),
            pltpu.VMEM((2, F, per, group, w), F32),
            pltpu.VMEM((full, wide), F32),
            pltpu.VMEM((full, wide), BF16),
            pltpu.VMEM((A, cw, wide), BF16),
            pltpu.VMEM((A, cw, wide), BF16),
            pltpu.VMEM((A, cw, wide), BF16),
            dma((F // 2, PIECES)),
            dma((F, PIECES)),
            dma((F // 2, PIECES)),
            dma((3, F)),
            dma((3, F)),
            dma((R,)),
            dma((R,)),
            dma((steps, R)),
            dma((steps, R)),
            dma((steps, R)),
            dma((steps, R)),
            dma((2, F)),
            dma((2, F)),
            dma((A,)),
            dma((A,)),
            dma((A,)),
            dma((A,)),
        ],
        compiler_params=pltpu.CompilerParams(
            collective_id=0, has_side_effects=True, vmem_limit_bytes=48 * 1024 * 1024
        ),
    )(
        slab_rows,
        labels.astype(F32)[None, :],
        mult,
        count,
        center_rows,
        theta_start,
        momentum,
        leap,
    )
    return theta, moment, hess.T


def solution(mesh):
    return jax.shard_map(
        shards,
        mesh=mesh,
        in_specs=(
            P("rows", "feat"),
            P("rows"),
            P("feat"),
            P(None, "feat"),
            P(None, "feat"),
            P(),
            P("rows"),
            P("rows"),
        ),
        out_specs=(P(None, "feat"), P(None, "feat"), P("feat", "rows")),
        check_vma=False,
    )
```

time: 465 us -> 104 us (0.22)
  waiting for transfers between devices: 358 us -> 0 us
  Pallas kernels: 0 us -> 94.6 us
  blocking collectives: 53 us -> 0 us
  between operations: 15.8 us -> 1.3 us
  matrix products: 11.6 us -> 0 us
  local copies, waits for them, and re-layouts: 14 us -> 5.94 us
  other arithmetic: 8.08 us -> 2.31 us
    psum x6 -> x0, waiting for transfers between devices: 266 us -> none  [the longest x3 214 us: gradient(): combined = lax.psum(summand, 'rows')]
    pallas_call x0 -> x1, Pallas kernels: none -> 94.6 us  [shards(): pl.pallas_call(functools.partial(kernel, R, F, S, whole_rows), out_shape=...]
    reduce_scatter x1 -> x0, waiting for transfers between devices: 87 us -> none  [shards(): lax.psum_scatter(hessian_block, 'rows', scatter_dimension=1, tiled=True)]
    psum x2 -> x0, blocking collectives: 30.3 us -> none  [the longest x1 21.9 us: shards(): grad_hat, sample_total = lax.psum((grad_local, count_float), 'rows')]
    all_gather x4 -> x0, blocking collectives: 22.7 us -> none  [the longest x3 17.5 us: gradient(): lax.all_gather(position.astype(jnp.bfloat16), 'feat', axis=1, tiled=True)]
    dot_general x12 -> x0, matrix products: 11.6 us -> none  [the longest x1 4.91 us: shards(): lax.dot_general(scaled, lax.all_gather(slab_rows, 'feat', axis=1, tiled=T...]
    gather x2 -> x0, local copies, waits for them, and re-layouts: 10.8 us -> none  [the longest x1 6.87 us: shards(): logit_ref = jnp.take(logit_hat, sample_index)]
    convert_element_type x8 -> x1, other arithmetic: 5.49 us -> 0.68 us  [shards(): labels.astype(F32)[None, :]]
  transfers between devices with their start and end apart: 8 -> 0, of which waited for: 7 -> 0; matrix products, arithmetic and copies ran while one was open for 4% -> 0% of each run, Pallas kernels for 0% -> 0%
where the time goes in v1:
time: 104 us
  Pallas kernels  94.6 us (91%)
  local copies, waits for them, and re-layouts  5.94 us (6%)
  other arithmetic  2.31 us (2%)
  between operations  1.3 us (1%)
    pallas_call x1, Pallas kernels, shards(): pl.pallas_call(functools.partial(kernel, R, F, S, whole_rows), out_shape=...  94.6 us
    unnamed x9, local copies, waits for them, and re-layouts  5.15 us

profile of v1, /device:TPU:0, one launch (start us, length us, event | category | flops | bytes accessed | tf_op | source)
XLA Modules:
  0.0 104.1 jit_solution(14737033048086927565)
XLA Ops:
  1.3 0.7 multiply_bitcast_fusion
  1.9 0.7 convert_element_type.9
  2.6 0.7 fusion
  3.3 0.3 convert_reduce_fusion
  3.6 0.1 copy.13.leap_ref
  3.7 0.7 broadcast_in_dim.34.center_ref
  4.4 0.0 copy-start
  4.4 1.0 copy-done
  5.4 0.0 copy-start.1
  5.4 0.9 copy-done.1
  6.3 0.0 copy-start.2
  6.3 0.9 copy-done.2
  7.2 94.6 %shard_map.103 = (f32[64,512]{1,0:T(8,128)S(1)}, f32[64,512]{1,0:T(8,128)S(1)}, f32[256,512]{1,0:T(8,128)S(1)}) custom-call(bf16[512,512]{1,0:T(8,128)(2,1)S(1)} %copy-done, f32[1,512]{1,0:T(1,128)S(1)} %bitcast.10, f32[1,512]{1,0:T(1,128)S(1)} %bitcast.9, f32[8,128]{1,0:T(8,128)S(1)} %broadcast_in_dim.33.count_ref, ...), custom_call_target="tpu_custom_call" | custom-call | tf_op jit(solution)/shard_map/pallas_call | solution.py:407
  101.8 1.0 copy.14
  102.8 0.7 copy.18
  103.5 0.7 copy.19
  (1 shorter events, 0.0 us)
Async XLA Ops:
  4.4 1.0 %copy-start = (bf16[512,512]{1,0:T(8,128)(2,1)S(1)}, bf16[512,512]{1,0:T(8,128)(2,1)}, u32[]{:S(2)}) copy-start(bf16[512,512]{1,0:T(8,128)(2,1)} %x_ref.1) | copy-start | bytes 1572868
  5.4 0.9 copy-start.1
  6.3 0.9 copy-start.2

commit v2 on v1

v2 whole, which is shorter than its diff:
```python
import functools
import math

import jax
import jax.numpy as jnp
from jax import lax
from jax.experimental import pallas as pl
from jax.experimental.pallas import tpu as pltpu
from jax.sharding import PartitionSpec as P

STEPS = 2
LANES = 128
PIECES = 4
MESH = pl.DeviceIdType.MESH
F32, BF16 = jnp.float32, jnp.bfloat16


def each(count, body, limit=8):
    if count <= limit:
        for number in range(count):
            body(number)
    else:
        lax.fori_loop(0, count, lambda number, none: (body(number), none)[1], 0)


def dot(left, right, left_dim, right_dim):
    return lax.dot_general(
        left, right, (((left_dim,), (right_dim,)), ((), ())), preferred_element_type=F32
    )


def split(value):
    high = value.astype(BF16)
    return high, (value - high.astype(F32)).astype(BF16)


def kernel(
    R, F, S, whole_rows,
    x_ref, label_ref, mult_ref, count_ref, center_ref, theta_ref, mom_ref, leap_ref,
    theta_out, mom_out, hess_out,
    x_full, theta_full, mom_full, logit_part, logit_full, count_full,
    c_send, c_recv, near, near_recv, state, state_recv, final_recv,
    scaled_ref, h_part, h_send, h_recv, h_send2, h_recv2, h_recv3,
    x_ssem, x_rsem, x_fsem, s_ssem, s_rsem, n_ssem, n_rsem,
    c_ssem, c_rsem, p_ssem, p_rsem, q_ssem, q_rsem, o_ssem, o_rsem,
    h_ssem, h_rsem, g_ssem, g_rsem, k_ssem, k_rsem,
):
    rows, wide = x_ref.shape
    group = theta_ref.shape[0] // F
    w = c_send.shape[-1]
    per = wide // w
    A = R // 2
    cw = hess_out.shape[0]
    r, f = lax.axis_index("rows"), lax.axis_index("feat")
    a, b = r // 2, lax.rem(r, 2)
    mate = f + 1 - 2 * lax.rem(f, 2)
    piece = rows // PIECES

    def copy(src, dst, ssem, rsem, row, feat):
        return pltpu.make_async_remote_copy(
            src_ref=src, dst_ref=dst, send_sem=ssem, recv_sem=rsem,
            device_id=(row, feat), device_id_type=MESH,
        )

    def row_peer(i):
        return lax.rem(r + i + 1, R)

    barrier = pltpu.get_barrier_semaphore()
    at_once = jnp.broadcast_to(center_ref[...], (8, wide))
    high, low = split(at_once)
    both = jnp.concatenate([high.astype(F32), low.astype(F32)], 0).astype(BF16)

    def greet_row(i):
        pl.semaphore_signal(barrier, inc=1, device_id=(row_peer(i), f), device_id_type=MESH)

    def greet_feat(i):
        pl.semaphore_signal(
            barrier, inc=1, device_id=(r, lax.rem(f + i + 1, F)), device_id_type=MESH
        )

    each(R - 1, greet_row)
    each(F - 1, greet_feat)
    logit_part[...] = dot(both, x_ref[...], 1, 1)
    pl.semaphore_wait(barrier, R + F - 2)

    def small(i, number):
        peer = lax.rem(f + i + 1, F)
        theirs = pl.ds(pl.multiple_of(peer * group, group), group)
        src = (logit_part, theta_ref.at[theirs], mom_ref.at[theirs])[number]
        dst = (logit_full, theta_full, mom_full)[number].at[f]
        return copy(src, dst, s_ssem.at[number, peer], s_rsem.at[number, f], r, peer)

    def small_in(i, number):
        peer = lax.rem(f + i + 1, F)
        dst = (logit_full, theta_full, mom_full)[number].at[peer]
        return copy(dst, dst, s_ssem.at[number, peer], s_rsem.at[number, peer], r, peer)

    def part(c):
        return pl.ds(c * piece, piece)

    def x_out(i, c):
        peer = mate if i == 0 else lax.rem(f + 2 * i, F)
        return copy(
            x_ref.at[part(c)], x_full.at[f, part(c)], x_ssem.at[i, c], x_rsem.at[f, c], r, peer
        )

    def x_in(block, c):
        dst = x_full.at[block, part(c)]
        return copy(dst, dst, x_ssem.at[0, c], x_rsem.at[block, c], r, mate)

    def x_forward(i, c):
        block = lax.rem(f + 2 * i, F)
        dst = x_full.at[block, part(c)]
        return copy(dst, dst, x_fsem.at[i, c], x_rsem.at[block, c], r, mate)

    def count_out(i):
        peer = row_peer(i)
        return copy(count_ref, count_full.at[r], n_ssem.at[peer], n_rsem.at[r], peer, f)

    def count_in(i):
        peer = row_peer(i)
        dst = count_full.at[peer]
        return copy(dst, dst, n_ssem.at[peer], n_rsem.at[peer], peer, f)

    for i in range(F - 1):
        small(i, 0).start()
    for c in range(PIECES):
        for i in range(1, F // 2):
            x_out(i, c).start()
        if c == 0:
            for i in range(F - 1):
                for number in range(1, 3):
                    small(i, number).start()
            each(R - 1, lambda i: count_out(i).start())
    for c in range(PIECES):
        x_out(0, c).start()

    mine = pl.ds(pl.multiple_of(f * group, group), group)
    logit_full[f] = logit_part[...]
    theta_full[f] = theta_ref[mine]
    mom_full[f] = mom_ref[mine]
    x_full[f] = x_ref[...]
    count_full[r] = count_ref[...]
    leap = leap_ref[mine, :]

    for i in range(F - 1):
        small_in(i, 0).wait_recv()

    at_center = jnp.zeros((16, rows), F32)
    for g in range(F):
        at_center += logit_full[g]
    logit_hat = at_center[:1]
    center_all = at_center[:1] + at_center[8:9]
    prob_hat = jax.nn.sigmoid(logit_hat)
    weight = prob_hat * (1.0 - prob_hat)
    residual = (label_ref[...].astype(F32) - prob_hat).astype(BF16).astype(F32)

    def c_out(e, i):
        peer = row_peer(i)
        return copy(
            c_send.at[e, lax.rem(peer, S)], c_recv.at[e, r], c_ssem.at[e, peer],
            c_rsem.at[e, r], peer, f,
        )

    def c_in(e, i):
        peer = row_peer(i)
        dst = c_recv.at[e, peer]
        return copy(dst, dst, c_ssem.at[e, peer], c_rsem.at[e, peer], peer, f)

    def on_owner(number, body):
        if S == R:
            body()
        else:
            pl.when(number < S)(body)

    def contribute(e, chunk_of):
        now = jnp.zeros((2 * group if e == 0 else group, rows), F32)
        for k in range(S):
            columns = x_full[k // per, :, (k % per) * w : (k % per + 1) * w]
            if e == 0:
                now += dot(jnp.concatenate(split(chunk_of(k)), 0), columns, 1, 1)
            else:
                now += dot(chunk_of(k), columns, 1, 1)
        logit_now = now[:group]
        offset = (now[:group] + now[group:] if e == 0 else now) - center_all
        remainder = prob_hat - jax.nn.sigmoid(logit_now) + weight * (logit_now - logit_hat)
        remainder = remainder.astype(BF16).astype(F32)
        coef = residual - weight * offset + mult_ratio * remainder
        high, low = split(coef)
        both = jnp.concatenate([high, low], 0)
        for g in range(F):
            value = dot(both, x_full[g], 1, 0)
            value = value[:group] + value[group:]
            for h in range(per):
                c_send[e, g * per + h] = value[:, h * w : (h + 1) * w].astype(BF16)

        def send(i):
            on_owner(row_peer(i), lambda: c_out(e, i).start())

        each(R - 1, send)

    def reduced(e):
        on_owner(r, lambda: each(R - 1, lambda i: c_in(e, i).wait_recv()))
        c_recv[e, r] = c_send[e, lax.rem(r, S)]
        return lax.fori_loop(0, R, lambda i, acc: acc + c_recv[e, i].astype(F32), jnp.zeros((group, w), F32))

    own = lax.rem(r, S)
    rounded = near, near_recv, p_ssem, p_rsem
    whole = state, state_recv, q_ssem, q_rsem

    def p_out(kind, e, i):
        peer = row_peer(i)
        source, target, ssem, rsem = kind
        return copy(source.at[e], target.at[e, own], ssem.at[e, peer], rsem.at[e, own], peer, f)

    def p_in(kind, e, i):
        peer = lax.rem(row_peer(i), S)
        _, target, ssem, rsem = kind
        dst = target.at[e, peer]
        return copy(dst, dst, ssem.at[e, peer], rsem.at[e, peer], row_peer(i), f)

    def spread(kind, e):
        each(R - 1, lambda i: p_out(kind, e, i).start())
        kind[1][e, own] = kind[0][e]

    def gathered(kind, e):
        def take(i):
            on_owner(row_peer(i), lambda: p_in(kind, e, i).wait_recv())

        each(R - 1, take)

    def h_out(pair):
        rows_there = pl.ds(pl.multiple_of((2 * pair + 1 - b) * cw, cw), cw)
        return copy(
            h_send.at[rows_there], h_recv.at[pair], h_ssem.at[pair], h_rsem.at[pair],
            2 * a + 1 - b, f,
        )

    def g_out(pair):
        return copy(
            h_send2.at[pair], h_recv2.at[pair], g_ssem.at[pair], g_rsem.at[pair],
            2 * (a + 1 - 2 * lax.rem(a, 2)) + b, f,
        )

    def k_out(pair):
        return copy(
            h_send2.at[pair], h_recv3.at[a], k_ssem.at[pair], k_rsem.at[a], 2 * pair + b, f
        )

    def k_in(pair):
        dst = h_recv3.at[pair]
        return copy(dst, dst, k_ssem.at[pair], k_rsem.at[pair], 2 * pair + b, f)

    def own_rows(pair):
        return pl.ds(pl.multiple_of((2 * pair + b) * cw, cw), cw)

    def alike(j):
        return lax.rem(a + 2 * j, A)

    many = A // F

    def block_at(i):
        return lax.rem((f if i % 2 == 0 else mate) + 2 * (i // 2), F)

    column = jnp.transpose(jnp.broadcast_to(weight, (LANES, rows)))[:, :1]
    scaled_ref[...] = (column * x_ref[...].astype(F32)).astype(BF16)

    def h_block(i):
        g = block_at(i)
        value = dot(x_full[g], scaled_ref[...], 0, 0)
        where = pl.ds(pl.multiple_of(g * wide, wide), wide)
        h_part[where, :] = value
        h_send[where, :] = value.astype(BF16)
        each(many, lambda j: h_out(g * many + j).start())

    def h_pass(i):
        def one(j):
            pair = block_at(i) * many + j
            h_out(pair).wait_recv()
            value = h_part[own_rows(pair), :] + h_recv[pair].astype(F32)

            @pl.when(lax.rem(pair, 2) == lax.rem(a, 2))
            def _():
                h_part[own_rows(pair), :] = value

            @pl.when(lax.rem(pair, 2) != lax.rem(a, 2))
            def _():
                h_send2[pair] = value.astype(BF16)
                g_out(pair).start()

        each(many, one)

    def h_across(j):
        pair = alike(j + 1)
        g_out(pair).wait_recv()
        value = h_part[own_rows(pair), :] + h_recv2[pair].astype(F32)
        h_send2[pair] = value.astype(BF16)
        k_out(pair).start()

    def o_out(number, i):
        peer = lax.rem(f + i + 1, F)
        theirs = pl.ds(peer * per, per)
        return copy(
            state_recv.at[number, theirs], final_recv.at[number, f], o_ssem.at[number, peer],
            o_rsem.at[number, f], r, peer,
        )

    def o_in(number, i):
        peer = lax.rem(f + i + 1, F)
        dst = final_recv.at[number, peer]
        return copy(dst, dst, o_ssem.at[number, peer], o_rsem.at[number, peer], r, peer)

    def finish(number):
        for i in range(F - 1):
            o_out(number, i).start()
        for h in range(per):
            final_recv[number, f, h] = state_recv[number, f * per + h]

    def write(number, out):
        for i in range(F - 1):
            o_in(number, i).wait_recv()
        for g in range(F):
            for h in range(per):
                out[g * group : (g + 1) * group, h * w : (h + 1) * w] = final_recv[number, g, h]

    def own_part(full):
        block = own // per
        if per == 1:
            return full[block]
        value = full[block, :, :w]
        for h in range(1, per):
            value = jnp.where(
                lax.rem(own, per) == h, full[block, :, h * w : (h + 1) * w], value
            )
        return value

    h_block(0)
    for c in range(PIECES):
        x_in(mate, c).wait_recv()
    h_block(1)
    for c in range(PIECES):
        for i in range(1, F // 2):
            x_in(lax.rem(f + 2 * i, F), c).wait_recv()
            x_forward(i, c).start()
    for i in range(F - 1):
        for number in range(1, 3):
            small_in(i, number).wait_recv()
    each(R - 1, lambda i: count_in(i).wait_recv())
    total = lax.fori_loop(0, R, lambda i, acc: acc + count_full[i], jnp.zeros_like(count_ref))
    mult_ratio = mult_ref[...] * (float(whole_rows) / total[:1, :1])
    for c in range(PIECES):
        for i in range(1, F // 2):
            x_in(lax.rem(mate + 2 * i, F), c).wait_recv()

    contribute(
        0, lambda k: theta_full[k // per, :, (k % per) * w : (k % per + 1) * w]
    )
    for i in range(2, F):
        h_block(i)
    position, moment = own_part(theta_full), own_part(mom_full)
    factor = 0.5 * leap
    for e in range(STEPS):
        moment = moment + factor * (reduced(e) - position)
        position = position + leap * moment
        factor = leap if e + 1 < STEPS else 0.5 * leap
        near[e] = position.astype(BF16)
        on_owner(r, functools.partial(spread, rounded, e))
        if e == STEPS - 1:
            state[0] = position
            on_owner(r, functools.partial(spread, whole, 0))
        gathered(rounded, e)
        contribute(e + 1, functools.partial(lambda k, e: near_recv[e, k], e=e))
        if e == STEPS - 1:
            gathered(whole, 0)
            finish(0)
        if e == 1:
            for i in range(F):
                h_pass(i)
    moment = moment + factor * (reduced(STEPS) - position)
    state[1] = moment
    on_owner(r, functools.partial(spread, whole, 1))
    each(A // 2 - 1, h_across)
    gathered(whole, 1)
    finish(1)
    write(0, theta_out)

    g_out(a).wait_recv()
    hess_out[...] = h_part[own_rows(a), :] + h_recv2[a].astype(F32)

    def h_add(j):
        pair = alike(j + 1)
        k_in(pair).wait_recv()
        hess_out[...] += h_recv3[pair].astype(F32)

    each(A // 2 - 1, h_add)
    write(1, mom_out)

    for c in range(PIECES):
        for i in range(F // 2):
            x_out(i, c).wait_send()
        for i in range(1, F // 2):
            x_forward(i, c).wait_send()
    for i in range(F - 1):
        for number in range(3):
            small(i, number).wait_send()
        for number in range(2):
            o_out(number, i).wait_send()
    each(R - 1, lambda i: count_out(i).wait_send())
    for e in range(STEPS + 1):
        each(
            R - 1,
            lambda i: on_owner(row_peer(i), lambda: c_out(e, i).wait_send()),
        )
    for e in range(STEPS):
        on_owner(r, lambda: each(R - 1, lambda i: p_out(rounded, e, i).wait_send()))
    for e in range(2):
        on_owner(r, lambda: each(R - 1, lambda i: p_out(whole, e, i).wait_send()))
    each(A, lambda pair: h_out(pair).wait_send())
    each(A // 2, lambda j: g_out(lax.rem(a + 1 + 2 * j, A)).wait_send())
    each(A // 2 - 1, lambda j: k_out(alike(j + 1)).wait_send())


def shards(slab_rows, labels, center, theta_start, momentum, step_size, sample_index, sample_count):
    R, F = lax.axis_size("rows"), lax.axis_size("feat")
    rows, wide = slab_rows.shape
    whole_rows = rows * R
    full = wide * F
    chains = theta_start.shape[0]
    group = chains // F
    S = min(R, full // LANES)
    w = full // S
    cw = full // R
    A = R // 2
    live = jnp.arange(sample_index.shape[0], dtype=jnp.int32) < sample_count[0]
    slot_row = jnp.where(live, sample_index, -1)
    mult = jnp.sum(
        (slot_row[:, None] == jnp.arange(rows, dtype=jnp.int32)[None, :]).astype(F32), axis=0
    )[None, :]
    count = jnp.broadcast_to(sample_count.astype(F32)[None, :], (8, LANES))
    leap = (step_size * math.sqrt(full / whole_rows))[:, None]
    vmem = pl.BlockSpec(memory_space=pltpu.VMEM)
    dma = pltpu.SemaphoreType.DMA
    steps = STEPS + 1
    per = wide // w
    theta, moment, hess = pl.pallas_call(
        functools.partial(kernel, R, F, S, whole_rows),
        out_shape=(
            jax.ShapeDtypeStruct((chains, wide), F32),
            jax.ShapeDtypeStruct((chains, wide), F32),
            jax.ShapeDtypeStruct((cw, wide), F32),
        ),
        in_specs=[vmem] * 8,
        out_specs=(vmem,) * 3,
        scratch_shapes=[
            pltpu.VMEM((F, rows, wide), BF16),
            pltpu.VMEM((F, group, wide), F32),
            pltpu.VMEM((F, group, wide), F32),
            pltpu.VMEM((16, rows), F32),
            pltpu.VMEM((F, 16, rows), F32),
            pltpu.VMEM((R, 8, LANES), F32),
            pltpu.VMEM((steps, S, group, w), BF16),
            pltpu.VMEM((steps, R, group, w), BF16),
            pltpu.VMEM((STEPS, group, w), BF16),
            pltpu.VMEM((STEPS, S, group, w), BF16),
            pltpu.VMEM((2, group, w), F32),
            pltpu.VMEM((2, S, group, w), F32),
            pltpu.VMEM((2, F, per, group, w), F32),
            pltpu.VMEM((rows, wide), BF16),
            pltpu.VMEM((full, wide), F32),
            pltpu.VMEM((full, wide), BF16),
            pltpu.VMEM((A, cw, wide), BF16),
            pltpu.VMEM((A, cw, wide), BF16),
            pltpu.VMEM((A, cw, wide), BF16),
            pltpu.VMEM((A, cw, wide), BF16),
            dma((F // 2, PIECES)),
            dma((F, PIECES)),
            dma((F // 2, PIECES)),
            dma((3, F)),
            dma((3, F)),
            dma((R,)),
            dma((R,)),
            dma((steps, R)),
            dma((steps, R)),
            dma((STEPS, R)),
            dma((STEPS, R)),
            dma((2, R)),
            dma((2, R)),
            dma((2, F)),
            dma((2, F)),
            dma((A,)),
            dma((A,)),
            dma((A,)),
            dma((A,)),
            dma((A,)),
            dma((A,)),
        ],
        compiler_params=pltpu.CompilerParams(
            collective_id=0, has_side_effects=True, vmem_limit_bytes=48 * 1024 * 1024
        ),
    )(
        slab_rows,
        labels[None, :],
        mult,
        count,
        center[None, :],
        theta_start,
        momentum,
        leap,
    )
    return theta, moment, hess.T


def solution(mesh):
    return jax.shard_map(
        shards,
        mesh=mesh,
        in_specs=(
            P("rows", "feat"),
            P("rows"),
            P("feat"),
            P(None, "feat"),
            P(None, "feat"),
            P(),
            P("rows"),
            P("rows"),
        ),
        out_specs=(P(None, "feat"), P(None, "feat"), P("feat", "rows")),
        check_vma=False,
    )
```

time: 104 us -> 85.3 us (0.82)
  Pallas kernels: 94.6 us -> 75.5 us
    pallas_call x1, Pallas kernels: 94.6 us -> 75.5 us  [shards(): pl.pallas_call(functools.partial(kernel, R, F, S, whole_rows), out_shape=...]
    unnamed x9 -> x13, local copies, waits for them, and re-layouts: 5.15 us -> 6.52 us
where the time goes in v2:
time: 85.3 us; the launch traced here: 85 us
  Pallas kernels  75.5 us (89%)
  local copies, waits for them, and re-layouts  6.62 us (8%)
  other arithmetic  1.63 us (2%)
  between operations  1.3 us (2%)
    pallas_call x1, Pallas kernels, shards(): pl.pallas_call(functools.partial(kernel, R, F, S, whole_rows), out_shape=...  75.5 us
    unnamed x13, local copies, waits for them, and re-layouts  6.52 us

profile of v2, /device:TPU:0, one launch (start us, length us, event | category | flops | bytes accessed | tf_op | source)
XLA Modules:
  0.0 85.0 jit_solution(1810103348209172690)
XLA Ops:
  1.3 0.7 multiply_bitcast_fusion
  1.9 0.7 fusion
  2.6 0.3 convert_reduce_fusion
  2.9 0.1 copy.13.leap_ref
  3.0 0.0 copy-start
  3.0 1.0 %copy-done = bf16[512,512]{1,0:T(8,128)(2,1)S(1)} copy-done((bf16[512,512]{1,0:T(8,128)(2,1)S(1)}, bf16[512,512]{1,0:T(8,128)(2,1)}, u32[]{:S(2)}) %copy-start) | copy-done | bytes 524312
  4.1 0.0 copy-start.1
  4.1 0.9 %copy-done.1 = f32[64,512]{1,0:T(8,128)S(1)} copy-done((f32[64,512]{1,0:T(8,128)S(1)}, f32[64,512]{1,0:T(8,128)}, u32[]{:S(2)}) %copy-start.1) | copy-done | bytes 131096
  5.0 0.0 copy-start.2
  5.0 0.9 %copy-done.2 = f32[64,512]{1,0:T(8,128)S(1)} copy-done((f32[64,512]{1,0:T(8,128)S(1)}, f32[64,512]{1,0:T(8,128)}, u32[]{:S(2)}) %copy-start.2) | copy-done | bytes 131096
  5.9 0.0 copy-start.3
  5.9 0.7 copy-done.3
  6.6 0.0 copy-start.4
  6.6 0.7 copy-done.4
  7.2 75.5 %shard_map.103 = (f32[64,512]{1,0:T(8,128)S(1)}, f32[64,512]{1,0:T(8,128)S(1)}, f32[256,512]{1,0:T(8,128)S(1)}) custom-call(bf16[512,512]{1,0:T(8,128)(2,1)S(1)} %copy-done, s32[1,512]{1,0:T(1,128)S(1)} %bitcast.11, f32[1,512]{1,0:T(1,128)S(1)} %bitcast.10, f32[8,128]{1,0:T(8,128)S(1)} %broadcast_in_dim.30.count_ref, f32[1,512]{1,0:T(1,128)S(1)} %bitcast.12, ...), custom_call_target="tpu_custom_call" | custom-call | tf_op jit(solution)/shard_map/pallas_call | solution.py:445
  82.7 1.0 %copy.14 = f32[512,256]{1,0:T(8,128)} copy(f32[512,256]{0,1:T(8,128)S(1)} %bitcast.9) | data formatting | bytes 1048576
  83.7 0.7 copy.18
  84.4 0.7 copy.19
  (1 shorter events, 0.0 us)
Async XLA Ops:
  3.0 1.0 %copy-start = (bf16[512,512]{1,0:T(8,128)(2,1)S(1)}, bf16[512,512]{1,0:T(8,128)(2,1)}, u32[]{:S(2)}) copy-start(bf16[512,512]{1,0:T(8,128)(2,1)} %x_ref.1) | copy-start | bytes 1572868
  4.1 0.9 %copy-start.1 = (f32[64,512]{1,0:T(8,128)S(1)}, f32[64,512]{1,0:T(8,128)}, u32[]{:S(2)}) copy-start(f32[64,512]{1,0:T(8,128)} %theta_ref.1) | copy-start | bytes 393220
  5.0 0.9 %copy-start.2 = (f32[64,512]{1,0:T(8,128)S(1)}, f32[64,512]{1,0:T(8,128)}, u32[]{:S(2)}) copy-start(f32[64,512]{1,0:T(8,128)} %mom_ref.1) | copy-start | bytes 393220
  5.9 0.7 copy-start.3
  6.6 0.7 copy-start.4

commit v3 on v2

--- a/solution.py
+++ b/solution.py
@@ -368,13 +368,16 @@
         if e == STEPS - 1:
             state[0] = position
             on_owner(r, functools.partial(spread, whole, 0))
+        if e == 1:
+            for i in range(F // 2):
+                h_pass(i)
         gathered(rounded, e)
         contribute(e + 1, functools.partial(lambda k, e: near_recv[e, k], e=e))
         if e == STEPS - 1:
             gathered(whole, 0)
             finish(0)
         if e == 1:
-            for i in range(F):
+            for i in range(F // 2, F):
                 h_pass(i)
     moment = moment + factor * (reduced(STEPS) - position)
     state[1] = moment

time: 85.3 us -> 84.3 us (0.988)
  Pallas kernels: 75.5 us -> 73.9 us
    pallas_call x1, Pallas kernels: 75.5 us -> 73.9 us  [shards(): pl.pallas_call(functools.partial(kernel, R, F, S, whole_rows), out_shape=...]
where the time goes in v3:
time: 84.3 us; the launch traced here: 83.5 us
  Pallas kernels  73.9 us (88%)
  local copies, waits for them, and re-layouts  6.62 us (8%)
  other arithmetic  1.63 us (2%)
  between operations  1.3 us (2%)
    pallas_call x1, Pallas kernels, shards(): pl.pallas_call(functools.partial(kernel, R, F, S, whole_rows), out_shape=...  73.9 us
    unnamed x13, local copies, waits for them, and re-layouts  6.52 us

profile of v3, /device:TPU:0, one launch (start us, length us, event | category | flops | bytes accessed | tf_op | source)
XLA Modules:
  0.0 83.5 jit_solution(14627414146990499511)
XLA Ops:
  1.3 0.7 multiply_bitcast_fusion
  1.9 0.7 fusion
  2.6 0.3 convert_reduce_fusion
  2.9 0.1 copy.13.leap_ref
  3.0 0.0 copy-start
  3.0 1.0 %copy-done = bf16[512,512]{1,0:T(8,128)(2,1)S(1)} copy-done((bf16[512,512]{1,0:T(8,128)(2,1)S(1)}, bf16[512,512]{1,0:T(8,128)(2,1)}, u32[]{:S(2)}) %copy-start) | copy-done | bytes 524312
  4.1 0.0 copy-start.1
  4.1 0.9 %copy-done.1 = f32[64,512]{1,0:T(8,128)S(1)} copy-done((f32[64,512]{1,0:T(8,128)S(1)}, f32[64,512]{1,0:T(8,128)}, u32[]{:S(2)}) %copy-start.1) | copy-done | bytes 131096
  5.0 0.0 copy-start.2
  5.0 0.9 %copy-done.2 = f32[64,512]{1,0:T(8,128)S(1)} copy-done((f32[64,512]{1,0:T(8,128)S(1)}, f32[64,512]{1,0:T(8,128)}, u32[]{:S(2)}) %copy-start.2) | copy-done | bytes 131096
  5.9 0.0 copy-start.3
  5.9 0.7 copy-done.3
  6.6 0.0 copy-start.4
  6.6 0.7 copy-done.4
  7.2 73.9 %shard_map.103 = (f32[64,512]{1,0:T(8,128)S(1)}, f32[64,512]{1,0:T(8,128)S(1)}, f32[256,512]{1,0:T(8,128)S(1)}) custom-call(bf16[512,512]{1,0:T(8,128)(2,1)S(1)} %copy-done, s32[1,512]{1,0:T(1,128)S(1)} %bitcast.11, f32[1,512]{1,0:T(1,128)S(1)} %bitcast.10, f32[8,128]{1,0:T(8,128)S(1)} %broadcast_in_dim.30.count_ref, f32[1,512]{1,0:T(1,128)S(1)} %bitcast.12, ...), custom_call_target="tpu_custom_call" | custom-call | tf_op jit(solution)/shard_map/pallas_call | solution.py:448
  81.2 1.0 %copy.14 = f32[512,256]{1,0:T(8,128)} copy(f32[512,256]{0,1:T(8,128)S(1)} %bitcast.9) | data formatting | bytes 1048576
  82.2 0.7 copy.18
  82.8 0.7 copy.19
  (1 shorter events, 0.0 us)
Async XLA Ops:
  3.0 1.0 %copy-start = (bf16[512,512]{1,0:T(8,128)(2,1)S(1)}, bf16[512,512]{1,0:T(8,128)(2,1)}, u32[]{:S(2)}) copy-start(bf16[512,512]{1,0:T(8,128)(2,1)} %x_ref.1) | copy-start | bytes 1572868
  4.1 0.9 %copy-start.1 = (f32[64,512]{1,0:T(8,128)S(1)}, f32[64,512]{1,0:T(8,128)}, u32[]{:S(2)}) copy-start(f32[64,512]{1,0:T(8,128)} %theta_ref.1) | copy-start | bytes 393220
  5.0 0.9 %copy-start.2 = (f32[64,512]{1,0:T(8,128)S(1)}, f32[64,512]{1,0:T(8,128)}, u32[]{:S(2)}) copy-start(f32[64,512]{1,0:T(8,128)} %mom_ref.1) | copy-start | bytes 393220
  5.9 0.7 copy-start.3
  6.6 0.7 copy-start.4
